TPU v7x, 256 devices: a whole 4x4x8 slice. The times are simulated.
256 devices in a mesh: tm: 4 (over y), height: 4 (over x), width: 16 (over z, core).
Axes of the slice: x: 4, y: 4, z: 8, core: 2. Of those that a mesh axis runs over, the one named last changes fastest.
Arguments:
- features: bfloat16 [16, 32, 160, 384], P('tm', 'height', 'width'), may hold values from -6 to 6
- first_gain: float32 [384], replicated, may hold values from 0.5 to 2
- first_kernel: bfloat16 [27, 384, 384], P(None, ('height', 'width')), may hold values from -0.0625 to 0.0625
- first_bias: float32 [384], replicated, may hold values from -3 to 3
- second_gain: float32 [384], replicated, may hold values from 0.5 to 2
- second_kernel: bfloat16 [27, 384, 384], P(None, ('height', 'width')), may hold values from -0.0625 to 0.0625
- second_bias: float32 [384], replicated, may hold values from -3 to 3
Outputs:
- block_out: bfloat16 [16, 32, 160, 384], P('tm', 'height', 'width')
All inputs are finite; a program needn't handle non-finite values.
Results may differ from a plain program's by a relative error of at most 0.012.
Values may be sent and summed in bfloat16 or wider, within the bound.
No kernel may reach another device: no remote copies, remote signals or barrier semaphores. Data moves between devices by JAX's collectives and lax.ppermute only.
A program may use at most 128 MiB of HBM per device.

v0:
```python
import jax
import jax.numpy as jnp
from jax import lax
from jax.sharding import PartitionSpec as P


def passed_along(x, axis, by):
    devices = lax.axis_size(axis)
    pairs = [(i, i + by) for i in range(devices) if 0 <= i + by < devices]
    return lax.ppermute(x, axis, pairs)


def extended(x, sides, width):
    for axis, dim in sides:
        devices, length = (lax.axis_size(axis), x.shape[dim])
        up = [(i, (i + 1) % devices) for i in range(devices - 1)]
        down = [(j, i) for i, j in up]
        last = lax.slice_in_dim(x, length - width, length, axis=dim)
        first = lax.slice_in_dim(x, 0, width, axis=dim)
        before = lax.ppermute(last, axis, up)
        after = lax.ppermute(first, axis, down)
        x = jnp.concatenate([before, x, after], axis=dim)
    return x


def activate(volume, gain):
    values = volume.astype(jnp.float32)
    square_mean = jnp.mean(values * values, axis=-1, keepdims=True)
    normed = values * lax.rsqrt(square_mean + 1e-06) * gain
    return jax.nn.silu(normed).astype(jnp.bfloat16)


def make_folder(widened, frames, rows, cols):

    def fold_piece(total, piece, start):
        count_in = piece.shape[1]
        for step_t in range(3):
            for step_h in range(3):
                for step_w in range(3):
                    window = widened[
                        step_t : step_t + frames, step_h : step_h + rows, step_w : step_w + cols
                    ]
                    total = total + jnp.dot(
                        window.reshape(-1, count_in),
                        piece[9 * step_t + 3 * step_h + step_w],
                        preferred_element_type=jnp.float32,
                    )
        return total

    return fold_piece


def convolve(widened, kernel, bias, frames, rows, cols):
    out_chans = kernel.shape[2]
    empty = jnp.zeros((frames * rows * cols, out_chans), jnp.float32)
    fold_piece = make_folder(widened, frames, rows, cols)
    row_kernel = lax.all_gather(kernel, "width", axis=1, tiled=True)
    total = fold_piece(
        empty, lax.all_gather(row_kernel, "height", axis=1, tiled=True), jnp.int32(0)
    )
    return total.reshape(frames, rows, cols, out_chans) + bias


def widen(active):
    earlier = passed_along(active[-2:], "tm", 1)
    tall = jnp.concatenate([earlier, active], axis=0)
    return extended(tall, (("height", 1), ("width", 2)), 1)


def on_device(
    features, first_gain, first_kernel, first_bias, second_gain, second_kernel, second_bias
):
    frames, rows, cols, chans = features.shape
    first_active = activate(features, first_gain)
    middle = convolve(widen(first_active), first_kernel, first_bias, frames, rows, cols).astype(
        jnp.bfloat16
    )
    second_active = activate(middle, second_gain)
    second_wide = widen(second_active)
    summed = convolve(
        second_wide, second_kernel, second_bias, frames, rows, cols
    ) + features.astype(jnp.float32)
    return summed.astype(jnp.bfloat16)


def solution(mesh):
    placed = (
        P("tm", "height", "width", None),
        P(),
        P(None, ("height", "width"), None),
        P(),
        P(),
        P(None, ("height", "width"), None),
        P(),
    )
    return jax.shard_map(
        on_device,
        mesh=mesh,
        in_specs=placed,
        out_specs=P("tm", "height", "width", None),
        check_vma=False,
    )
```

profile of v0, /device:TPU:1, one launch (start us, length us, event | category | flops | bytes accessed | tf_op | source)
XLA Modules:
  0.0 329.2 jit_solution(13650596367216335500)
XLA Ops:
  8.1 45.3 %all-gather.5.cloned.1.call-done = bf16[27,96,384]{2,0,1:T(8,128)(2,1)} async-done(((bf16[27,6,384]{2,0,1:T(8,128)(2,1)}), bf16[27,96,384]{2,0,1:T(8,128)(2,1)}) %all-gather.5.cloned.1.call-update) | async-done | bytes 1990672 | tf_op jit(solution)/shard_map/all_gather | solution.py:57
  53.4 3.7 %copy.15 = bf16[27,96,384]{2,1,0:T(8,128)(2,1)} copy(bf16[27,96,384]{2,0,1:T(8,128)(2,1)} %all-gather.5.cloned.1.call-done) | data formatting | bytes 3981312 | tf_op jit(solution)/shard_map/all_gather | solution.py:57
  57.1 36.5 %all-gather.9.cloned.1.call-done = bf16[27,96,384]{2,0,1:T(8,128)(2,1)} async-done(((bf16[27,6,384]{2,0,1:T(8,128)(2,1)}), bf16[27,96,384]{2,0,1:T(8,128)(2,1)}) %all-gather.9.cloned.1.call-update) | async-done | bytes 1990672 | tf_op jit(solution)/shard_map/all_gather | solution.py:57
  93.6 3.7 %copy.16 = bf16[27,96,384]{2,1,0:T(8,128)(2,1)} copy(bf16[27,96,384]{2,0,1:T(8,128)(2,1)} %all-gather.9.cloned.1.call-done) | data formatting | bytes 3981312 | tf_op jit(solution)/shard_map/all_gather | solution.py:57
  97.9 3.1 collective-permute-start
  101.8 3.2 collective-permute-done
  106.3 4.0 %collective-permute-start.1 = (bf16[6,1,10,384]{3,2,1,0:T(8,128)(2,1)S(1)}, bf16[6,1,10,384]{3,2,1,0:T(8,128)(2,1)S(1)}, u32[]{:S(2)}, u32[]{:S(2)}) collective-permute-start(bf16[6,1,10,384]{3,2,1,0:T(8,128)(2,1)S(1)} %get-tuple-element.71), channel_id=1, source_target_pairs={{0,16},{16,32},{32,48},{1,17},{17,33},{33,49},{2,18},{18,34},{34,5... | collective-permute-start | bytes 138248 | tf_op jit(solution)/shard_map/ppermute | solution.py:20
  114.2 4.9 %collective-permute-start.3 = (bf16[6,10,1,384]{3,2,1,0:T(2,128)(2,1)}, bf16[6,10,1,384]{3,2,1,0:T(2,128)(2,1)S(1)}, u32[]{:S(2)}, u32[]{:S(2)}) collective-permute-start(bf16[6,10,1,384]{3,2,1,0:T(2,128)(2,1)} %get-tuple-element.47), channel_id=1, source_target_pairs={{0,1},{1,2},{2,3},{3,4},{4,5},{5,6},{6,7},{7,8},{8,9},{9,10},{10,1... | collective-permute-start | bytes 138248 | tf_op jit(solution)/shard_map/ppermute | solution.py:20
  119.1 2.1 collective-permute-start.4
  127.2 2.3 fusion.32
  129.4 1.8 reshape.211
  133.0 1.8 reshape.199
  134.8 1.8 reshape.200
  136.6 1.8 reshape.202
  140.2 1.8 reshape.205
  142.0 1.8 reshape.206
  151.7 24.5 %all-gather.7.cloned.1.call-done = bf16[27,384,384]{2,1,0:T(8,128)(2,1)} async-done(((bf16[27,96,384]{2,1,0:T(8,128)(2,1)}), bf16[27,384,384]{2,1,0:T(8,128)(2,1)}) %all-gather.7.cloned.1.call-update) | async-done | bytes 7962640 | tf_op jit(solution)/shard_map/all_gather | solution.py:59
  194.3 3.3 collective-permute-start.5
  197.6 3.5 %collective-permute-done.5 = bf16[2,8,10,384]{3,2,1,0:T(8,128)(2,1)S(1)} collective-permute-done((bf16[2,8,10,384]{3,2,1,0:T(8,128)(2,1)S(1)}, bf16[2,8,10,384]{3,2,1,0:T(8,128)(2,1)S(1)}, u32[]{:S(2)}, u32[]{:S(2)}) %collective-permute-start.5) | collective-permute-done | bytes 122912 | tf_op jit(solution)/shard_map/ppermute | solution.py:10
  202.5 4.2 %collective-permute-start.6 = (bf16[6,1,10,384]{3,2,1,0:T(8,128)(2,1)S(1)}, bf16[6,1,10,384]{3,2,1,0:T(8,128)(2,1)S(1)}, u32[]{:S(2)}, u32[]{:S(2)}) collective-permute-start(bf16[6,1,10,384]{3,2,1,0:T(8,128)(2,1)S(1)} %get-tuple-element.65), channel_id=1, source_target_pairs={{0,16},{16,32},{32,48},{1,17},{17,33},{33,49},{2,18},{18,34},{34,5... | collective-permute-start | bytes 138248 | tf_op jit(solution)/shard_map/ppermute | solution.py:20
  210.1 5.8 %collective-permute-start.8 = (bf16[6,10,1,384]{3,2,1,0:T(2,128)(2,1)}, bf16[6,10,1,384]{3,2,1,0:T(2,128)(2,1)}, u32[]{:S(2)}, u32[]{:S(2)}) collective-permute-start(bf16[6,10,1,384]{3,2,1,0:T(2,128)(2,1)} %get-tuple-element.25), channel_id=1, source_target_pairs={{0,1},{1,2},{2,3},{3,4},{4,5},{5,6},{6,7},{7,8},{8,9},{9,10},{10,1... | collective-permute-start | bytes 138248 | tf_op jit(solution)/shard_map/ppermute | solution.py:20
  215.9 1.9 collective-permute-start.9
  220.1 42.1 %all-gather.11.cloned.1.call-done = bf16[27,384,384]{2,1,0:T(8,128)(2,1)} async-done(((bf16[27,96,384]{2,1,0:T(8,128)(2,1)}), bf16[27,384,384]{2,1,0:T(8,128)(2,1)}) %all-gather.11.cloned.1.call-update) | async-done | bytes 7962640 | tf_op jit(solution)/shard_map/all_gather | solution.py:59
  268.8 1.8 reshape.249
  275.7 1.9 fusion.31
  277.6 1.9 reshape.225
  279.4 1.8 reshape.227
  281.2 1.8 reshape.228
  284.8 1.8 reshape.231
  293.7 1.8 reshape.240
  295.5 1.8 reshape.242
  297.3 1.8 reshape.243
  (218 shorter events, 93.7 us)
Async XLA Ops:
  6.5 90.8 %copy-start.1 = (bf16[4,8,10,384]{3,1,2,0:T(8,128)(2,1)S(1)}, bf16[4,8,10,384]{3,1,2,0:T(8,128)(2,1)}, u32[]{:S(2)}) copy-start(bf16[4,8,10,384]{3,1,2,0:T(8,128)(2,1)} %param.7) | copy-start | bytes 737284
  6.5 91.0 %copy-start.35 = (f32[384]{0:T(512)S(1)}, f32[384]{0:T(512)}, u32[]{:S(2)}) copy-start(f32[384]{0:T(512)} %param.8) | copy-start | bytes 4612
  6.5 46.8 %all-gather.5.cloned.1.call-start = ((), (), s32[]{:S(2)}) async-start(), calls=%async_computation | async-start | bytes 2506752 | tf_op jit(solution)/shard_map/all_gather | solution.py:57
  7.3 86.4 %all-gather.9.cloned.1.call-start = ((), (), s32[]{:S(2)}) async-start(), calls=%async_computation.2 | async-start | bytes 2506752 | tf_op jit(solution)/shard_map/all_gather | solution.py:57
  8.0 168.2 %all-gather.7.cloned.1.call-start = ((), (), s32[]{:S(2)}) async-start(), calls=%async_computation.1 | async-start | bytes 9953280 | tf_op jit(solution)/shard_map/all_gather | solution.py:59
  57.1 205.1 %all-gather.11.cloned.1.call-start = ((), (), s32[]{:S(2)}) async-start(), calls=%async_computation.3 | async-start | bytes 9953280 | tf_op jit(solution)/shard_map/all_gather | solution.py:59
  97.9 7.1 %collective-permute-start = (bf16[2,8,10,384]{3,2,1,0:T(8,128)(2,1)S(1)}, bf16[2,8,10,384]{3,2,1,0:T(8,128)(2,1)S(1)}, u32[]{:S(2)}, u32[]{:S(2)}) collective-permute-start(bf16[2,8,10,384]{3,2,1,0:T(8,128)(2,1)S(1)} %slice.512), channel_id=1, source_target_pairs={{0,64},{64,128},{128,192},{1,65},{65,129},{129,193},{2,66},{66,130... | collective-permute-start | bytes 368648 | tf_op jit(solution)/shard_map/ppermute | solution.py:10
  105.0 7.0 %collective-permute-start.2 = (bf16[6,1,10,384]{3,2,1,0:T(8,128)(2,1)S(1)}, bf16[6,1,10,384]{3,2,1,0:T(8,128)(2,1)S(1)}, u32[]{:S(2)}, u32[]{:S(2)}) collective-permute-start(bf16[6,1,10,384]{3,2,1,0:T(8,128)(2,1)S(1)} %get-tuple-element.72), channel_id=1, source_target_pairs={{16,0},{32,16},{48,32},{17,1},{33,17},{49,33},{18,2},{34,18},{50,3... | collective-permute-start | bytes 138248 | tf_op jit(solution)/shard_map/ppermute | solution.py:21
  106.3 7.0 %collective-permute-start.1 = (bf16[6,1,10,384]{3,2,1,0:T(8,128)(2,1)S(1)}, bf16[6,1,10,384]{3,2,1,0:T(8,128)(2,1)S(1)}, u32[]{:S(2)}, u32[]{:S(2)}) collective-permute-start(bf16[6,1,10,384]{3,2,1,0:T(8,128)(2,1)S(1)} %get-tuple-element.71), channel_id=1, source_target_pairs={{0,16},{16,32},{32,48},{1,17},{17,33},{33,49},{2,18},{18,34},{34,5... | collective-permute-start | bytes 138248 | tf_op jit(solution)/shard_map/ppermute | solution.py:20
  114.2 12.3 %collective-permute-start.3 = (bf16[6,10,1,384]{3,2,1,0:T(2,128)(2,1)}, bf16[6,10,1,384]{3,2,1,0:T(2,128)(2,1)S(1)}, u32[]{:S(2)}, u32[]{:S(2)}) collective-permute-start(bf16[6,10,1,384]{3,2,1,0:T(2,128)(2,1)} %get-tuple-element.47), channel_id=1, source_target_pairs={{0,1},{1,2},{2,3},{3,4},{4,5},{5,6},{6,7},{7,8},{8,9},{9,10},{10,1... | collective-permute-start | bytes 138248 | tf_op jit(solution)/shard_map/ppermute | solution.py:20
  119.1 7.4 %collective-permute-start.4 = (bf16[6,10,1,384]{3,2,1,0:T(2,128)(2,1)}, bf16[6,10,1,384]{3,2,1,0:T(2,128)(2,1)S(1)}, u32[]{:S(2)}, u32[]{:S(2)}) collective-permute-start(bf16[6,10,1,384]{3,2,1,0:T(2,128)(2,1)} %get-tuple-element.48), channel_id=1, source_target_pairs={{1,0},{2,1},{3,2},{4,3},{5,4},{6,5},{7,6},{8,7},{9,8},{10,9},{11,1... | collective-permute-start | bytes 138248 | tf_op jit(solution)/shard_map/ppermute | solution.py:21
  148.1 35.8 %copy-start.7 = (bf16[320,384]{1,0:T(8,128)(2,1)S(1)}, bf16[320,384]{1,0:T(8,128)(2,1)}, u32[]{:S(2)}) copy-start(bf16[320,384]{1,0:T(8,128)(2,1)} %reshape.201) | copy-start | bytes 737284
  148.9 37.1 %copy-start.14 = (bf16[320,384]{1,0:T(8,128)(2,1)S(1)}, bf16[320,384]{1,0:T(8,128)(2,1)}, u32[]{:S(2)}) copy-start(bf16[320,384]{1,0:T(8,128)(2,1)} %reshape.204) | copy-start | bytes 737284
  151.4 36.3 %copy-start.26 = (bf16[320,384]{1,0:T(8,128)(2,1)S(1)}, bf16[320,384]{1,0:T(8,128)(2,1)}, u32[]{:S(2)}) copy-start(bf16[320,384]{1,0:T(8,128)(2,1)} %reshape.206) | copy-start | bytes 737284
  151.5 33.8 %copy-start.31 = (bf16[320,384]{1,0:T(8,128)(2,1)S(1)}, bf16[320,384]{1,0:T(8,128)(2,1)}, u32[]{:S(2)}) copy-start(bf16[320,384]{1,0:T(8,128)(2,1)} %reshape.202) | copy-start | bytes 737284
  151.5 34.2 %copy-start.29 = (bf16[320,384]{1,0:T(8,128)(2,1)S(1)}, bf16[320,384]{1,0:T(8,128)(2,1)}, u32[]{:S(2)}) copy-start(bf16[320,384]{1,0:T(8,128)(2,1)} %reshape.203) | copy-start | bytes 737284
  176.2 11.9 %copy-start.12 = (bf16[320,384]{1,0:T(8,128)(2,1)S(1)}, bf16[320,384]{1,0:T(8,128)(2,1)}, u32[]{:S(2)}) copy-start(bf16[320,384]{1,0:T(8,128)(2,1)} %reshape.207) | copy-start | bytes 737284
  177.8 10.7 %copy-start.25 = (bf16[320,384]{1,0:T(8,128)(2,1)S(1)}, bf16[320,384]{1,0:T(8,128)(2,1)}, u32[]{:S(2)}) copy-start(bf16[320,384]{1,0:T(8,128)(2,1)} %reshape.208) | copy-start | bytes 737284
  194.3 6.8 %collective-permute-start.5 = (bf16[2,8,10,384]{3,2,1,0:T(8,128)(2,1)S(1)}, bf16[2,8,10,384]{3,2,1,0:T(8,128)(2,1)S(1)}, u32[]{:S(2)}, u32[]{:S(2)}) collective-permute-start(bf16[2,8,10,384]{3,2,1,0:T(8,128)(2,1)S(1)} %slice.566), channel_id=1, source_target_pairs={{0,64},{64,128},{128,192},{1,65},{65,129},{129,193},{2,66},{66,130... | collective-permute-start | bytes 368648 | tf_op jit(solution)/shard_map/ppermute | solution.py:10
  201.2 7.2 %collective-permute-start.7 = (bf16[6,1,10,384]{3,2,1,0:T(8,128)(2,1)S(1)}, bf16[6,1,10,384]{3,2,1,0:T(8,128)(2,1)S(1)}, u32[]{:S(2)}, u32[]{:S(2)}) collective-permute-start(bf16[6,1,10,384]{3,2,1,0:T(8,128)(2,1)S(1)} %get-tuple-element.66), channel_id=1, source_target_pairs={{16,0},{32,16},{48,32},{17,1},{33,17},{49,33},{18,2},{34,18},{50,3... | collective-permute-start | bytes 138248 | tf_op jit(solution)/shard_map/ppermute | solution.py:21
  202.5 6.8 %collective-permute-start.6 = (bf16[6,1,10,384]{3,2,1,0:T(8,128)(2,1)S(1)}, bf16[6,1,10,384]{3,2,1,0:T(8,128)(2,1)S(1)}, u32[]{:S(2)}, u32[]{:S(2)}) collective-permute-start(bf16[6,1,10,384]{3,2,1,0:T(8,128)(2,1)S(1)} %get-tuple-element.65), channel_id=1, source_target_pairs={{0,16},{16,32},{32,48},{1,17},{17,33},{33,49},{2,18},{18,34},{34,5... | collective-permute-start | bytes 138248 | tf_op jit(solution)/shard_map/ppermute | solution.py:20
  210.1 60.4 %collective-permute-start.8 = (bf16[6,10,1,384]{3,2,1,0:T(2,128)(2,1)}, bf16[6,10,1,384]{3,2,1,0:T(2,128)(2,1)}, u32[]{:S(2)}, u32[]{:S(2)}) collective-permute-start(bf16[6,10,1,384]{3,2,1,0:T(2,128)(2,1)} %get-tuple-element.25), channel_id=1, source_target_pairs={{0,1},{1,2},{2,3},{3,4},{4,5},{5,6},{6,7},{7,8},{8,9},{9,10},{10,1... | collective-permute-start | bytes 138248 | tf_op jit(solution)/shard_map/ppermute | solution.py:20
  215.9 54.6 %collective-permute-start.9 = (bf16[6,10,1,384]{3,2,1,0:T(2,128)(2,1)}, bf16[6,10,1,384]{3,2,1,0:T(2,128)(2,1)}, u32[]{:S(2)}, u32[]{:S(2)}) collective-permute-start(bf16[6,10,1,384]{3,2,1,0:T(2,128)(2,1)} %get-tuple-element.26), channel_id=1, source_target_pairs={{1,0},{2,1},{3,2},{4,3},{5,4},{6,5},{7,6},{8,7},{9,8},{10,9},{11,1... | collective-permute-start | bytes 138248 | tf_op jit(solution)/shard_map/ppermute | solution.py:21
  277.6 22.3 %copy-start.3 = (bf16[4,8,10,384]{3,2,1,0:T(8,128)(2,1)S(1)}, bf16[4,8,10,384]{3,2,1,0:T(8,128)(2,1)}, u32[]{:S(2)}) copy-start(bf16[4,8,10,384]{3,2,1,0:T(8,128)(2,1)} %get-tuple-element.15) | copy-start | bytes 737284
  277.6 22.5 %copy-start.2 = (bf16[4,8,10,384]{3,2,1,0:T(8,128)(2,1)S(1)}, bf16[4,8,10,384]{3,2,1,0:T(8,128)(2,1)}, u32[]{:S(2)}) copy-start(bf16[4,8,10,384]{3,2,1,0:T(8,128)(2,1)} %get-tuple-element.14) | copy-start | bytes 737284
  299.9 13.8 %copy-start.30 = (bf16[320,384]{1,0:T(8,128)(2,1)S(1)}, bf16[320,384]{1,0:T(8,128)(2,1)}, u32[]{:S(2)}) copy-start(bf16[320,384]{1,0:T(8,128)(2,1)} %reshape.234) | copy-start | bytes 737284
  300.1 15.0 %copy-start.13 = (bf16[320,384]{1,0:T(8,128)(2,1)S(1)}, bf16[320,384]{1,0:T(8,128)(2,1)}, u32[]{:S(2)}) copy-start(bf16[320,384]{1,0:T(8,128)(2,1)} %reshape.235) | copy-start | bytes 737284
  300.3 16.1 %slice-start = ((s8[7962624]{0:T(1024)(128)(4,1)}), s8[4194304]{0:T(1024)(128)(4,1)S(1)}, s32[]{:S(2)}) async-start(s8[7962624]{0:T(1024)(128)(4,1)} %bitcast.217), calls=%async_computation.4 | async-start | bytes 8388608
  300.3 16.1 %copy-start.28 = (bf16[320,384]{1,0:T(8,128)(2,1)S(1)}, bf16[320,384]{1,0:T(8,128)(2,1)}, u32[]{:S(2)}) copy-start(bf16[320,384]{1,0:T(8,128)(2,1)} %reshape.236) | copy-start | bytes 737284
  303.3 13.4 %copy-start.27 = (bf16[320,384]{1,0:T(8,128)(2,1)S(1)}, bf16[320,384]{1,0:T(8,128)(2,1)}, u32[]{:S(2)}) copy-start(bf16[320,384]{1,0:T(8,128)(2,1)} %reshape.237) | copy-start | bytes 737284
  304.8 12.3 %copy-start.32 = (bf16[320,384]{1,0:T(8,128)(2,1)S(1)}, bf16[320,384]{1,0:T(8,128)(2,1)}, u32[]{:S(2)}) copy-start(bf16[320,384]{1,0:T(8,128)(2,1)} %reshape.238) | copy-start | bytes 737284
  306.2 11.2 %copy-start.24 = (bf16[320,384]{1,0:T(8,128)(2,1)S(1)}, bf16[320,384]{1,0:T(8,128)(2,1)}, u32[]{:S(2)}) copy-start(bf16[320,384]{1,0:T(8,128)(2,1)} %reshape.240) | copy-start | bytes 737284
  (22 other events, 122.8 us)
Sparse Core Ops, SparseCore 0:
  9.2 44.1 all-gather.4
  55.2 38.3 all-gather.8
  95.4 80.7 all-gather.6
  177.9 84.2 all-gather.10
where the time goes:
time: 331 us; the launch traced here: 329 us
  waiting for transfers between devices  159 us (48%)
  local copies, waits for them, and re-layouts  79.1 us (24%)
  matrix products  39.5 us (12%)
  starting transfers between devices  32 us (10%)
  between operations  14.3 us (4%)
  other arithmetic  5.48 us (2%)
    all_gather x2, waiting for transfers between devices, convolve(): row_kernel = lax.all_gather(kernel, 'width', axis=1, tiled=True)  81.8 us
    all_gather x2, waiting for transfers between devices, convolve(): lax.all_gather(row_kernel, 'height', axis=1, tiled=True)  66.6 us
    reshape x53, local copies, waits for them, and re-layouts, fold_piece(): window.reshape(-1, count_in)  63 us
    dot_general x54, matrix products, fold_piece(): jnp.dot(window.reshape(-1, count_in), piece[9 * step_t + 3 * step_h + ste...  39.5 us
    ppermute x4, starting transfers between devices, extended(): before = lax.ppermute(last, axis, up)  18.9 us
    slice x6, local copies, waits for them, and re-layouts, fold_piece(): widened[step_t:step_t + frames, step_h:step_h + rows, step_w:step_w + cols]  7.5 us
    all_gather x2, local copies, waits for them, and re-layouts, convolve(): row_kernel = lax.all_gather(kernel, 'width', axis=1, tiled=True)  7.38 us
    ppermute x2, waiting for transfers between devices, passed_along(): return lax.ppermute(x, axis, pairs)  6.76 us
  transfers between devices with their start and end apart: 14, of which 8 were waited for; matrix products, arithmetic and copies ran while one was open for 22% of the time, Pallas kernels for 0%

commit v1 on v0

--- a/solution.py
+++ b/solution.py
@@ -54,7 +54,15 @@
     out_chans = kernel.shape[2]
     empty = jnp.zeros((frames * rows * cols, out_chans), jnp.float32)
     fold_piece = make_folder(widened, frames, rows, cols)
-    row_kernel = lax.all_gather(kernel, "width", axis=1, tiled=True)
+    ways, here = (lax.axis_size("width"), lax.axis_index("width"))
+    grown, reach = (kernel, 1)
+    while reach < ways:
+        theirs = lax.ppermute(grown, "width", [(d, d ^ reach) for d in range(ways)])
+        mine_first = jnp.concatenate([grown, theirs], axis=1)
+        theirs_first = jnp.concatenate([theirs, grown], axis=1)
+        grown = jnp.where(here & reach == 0, mine_first, theirs_first)
+        reach = 2 * reach
+    row_kernel = grown
     total = fold_piece(
         empty, lax.all_gather(row_kernel, "height", axis=1, tiled=True), jnp.int32(0)
     )

time: 331 us -> 353 us (1.066)
  starting transfers between devices: 32 us -> 46 us
  local copies, waits for them, and re-layouts: 79.1 us -> 69.4 us
  waiting for transfers between devices: 159 us -> 166 us
  other arithmetic: 5.48 us -> 11.9 us
    ppermute x0 -> x8, waiting for transfers between devices: none -> 155 us  [convolve(): theirs = lax.ppermute(grown, 'width', [(d, d ^ reach) for d in range(ways)])]
    all_gather x2 -> x0, waiting for transfers between devices: 81.8 us -> none  [convolve(): row_kernel = lax.all_gather(kernel, 'width', axis=1, tiled=True)]
    all_gather x2, waiting for transfers between devices: 66.6 us -> 0.02 us  [convolve(): lax.all_gather(row_kernel, 'height', axis=1, tiled=True)]
    ppermute x0 -> x8, starting transfers between devices: none -> 16.4 us  [convolve(): theirs = lax.ppermute(grown, 'width', [(d, d ^ reach) for d in range(ways)])]
    ppermute x4, starting transfers between devices: 18.9 us -> 10.2 us  [extended(): before = lax.ppermute(last, axis, up)]
    all_gather x2 -> x0, local copies, waits for them, and re-layouts: 7.38 us -> none  [convolve(): row_kernel = lax.all_gather(kernel, 'width', axis=1, tiled=True)]
    select_n x0 -> x8, other arithmetic: none -> 5.46 us  [convolve(): grown = jnp.where(here & reach == 0, mine_first, theirs_first)]
    ppermute x4, starting transfers between devices: 6.61 us -> 11.8 us  [extended(): after = lax.ppermute(first, axis, down)]
  transfers between devices with their start and end apart: 14 -> 20, of which waited for: 8 -> 12; matrix products, arithmetic and copies ran while one was open for 22% -> 19% of each run, Pallas kernels for 0% -> 0%
where the time goes in v1:
time: 353 us; the launch traced here: 350 us
  waiting for transfers between devices  166 us (47%)
  local copies, waits for them, and re-layouts  69.4 us (20%)
  starting transfers between devices  46 us (13%)
  matrix products  41.8 us (12%)
  between operations  14.6 us (4%)
  other arithmetic  11.9 us (3%)
    ppermute x8, waiting for transfers between devices, convolve(): theirs = lax.ppermute(grown, 'width', [(d, d ^ reach) for d in range(ways)])  155 us
    reshape x53, local copies, waits for them, and re-layouts, fold_piece(): window.reshape(-1, count_in)  59.5 us
    dot_general x54, matrix products, fold_piece(): jnp.dot(window.reshape(-1, count_in), piece[9 * step_t + 3 * step_h + ste...  41.8 us
    ppermute x8, starting transfers between devices, convolve(): theirs = lax.ppermute(grown, 'width', [(d, d ^ reach) for d in range(ways)])  16.4 us
    ppermute x4, starting transfers between devices, extended(): after = lax.ppermute(first, axis, down)  11.8 us
    ppermute x4, starting transfers between devices, extended(): before = lax.ppermute(last, axis, up)  10.2 us
    ppermute x2, starting transfers between devices, passed_along(): return lax.ppermute(x, axis, pairs)  7.49 us
    ppermute x2, waiting for transfers between devices, passed_along(): return lax.ppermute(x, axis, pairs)  7.41 us
  transfers between devices with their start and end apart: 20, of which 12 were waited for; matrix products, arithmetic and copies ran while one was open for 19% of the time, Pallas kernels for 0%

profile of v1, /device:TPU:1, one launch (start us, length us, event | category | flops | bytes accessed | tf_op | source)
XLA Modules:
  0.0 350.2 jit_solution(16398536211608888795)
XLA Ops:
  7.5 3.3 collective-permute-start.4
  12.2 9.0 %collective-permute-done.5 = bf16[27,12,384]{2,1,0:T(8,128)(2,1)S(1)} collective-permute-done((bf16[27,12,384]{2,1,0:T(8,128)(2,1)S(1)}, bf16[27,12,384]{2,1,0:T(8,128)(2,1)S(1)}, u32[]{:S(2)}, u32[]{:S(2)}) %collective-permute-start.5) | collective-permute-done | bytes 248864 | tf_op jit(solution)/shard_map/ppermute | solution.py:60
  23.3 22.9 %collective-permute-done.6 = bf16[27,24,384]{2,1,0:T(8,128)(2,1)S(1)} collective-permute-done((bf16[27,24,384]{2,1,0:T(8,128)(2,1)S(1)}, bf16[27,24,384]{2,1,0:T(8,128)(2,1)S(1)}, u32[]{:S(2)}, u32[]{:S(2)}) %collective-permute-start.6) | collective-permute-done | bytes 497696 | tf_op jit(solution)/shard_map/ppermute | solution.py:60
  46.5 5.1 %collective-permute-start.7 = (bf16[27,48,384]{2,1,0:T(8,128)(2,1)S(1)}, bf16[27,48,384]{2,1,0:T(8,128)(2,1)S(1)}, u32[]{:S(2)}, u32[]{:S(2)}) collective-permute-start(bf16[27,48,384]{2,1,0:T(8,128)(2,1)S(1)} %maximum_select_fusion.2), channel_id=1, source_target_pairs={{0,8},{1,9},{2,10},{3,11},{4,12},{5,13},{6,14},{7,15},{8,0},{9,1},... | collective-permute-start | bytes 2985992 | tf_op jit(solution)/shard_map/ppermute | solution.py:60
  51.6 43.2 %collective-permute-done.7 = bf16[27,48,384]{2,1,0:T(8,128)(2,1)S(1)} collective-permute-done((bf16[27,48,384]{2,1,0:T(8,128)(2,1)S(1)}, bf16[27,48,384]{2,1,0:T(8,128)(2,1)S(1)}, u32[]{:S(2)}, u32[]{:S(2)}) %collective-permute-start.7) | collective-permute-done | bytes 995360 | tf_op jit(solution)/shard_map/ppermute | solution.py:60
  94.7 1.8 maximum_select_fusion
  96.7 1.8 collective-permute-start.13
  99.9 9.0 %collective-permute-done.14 = bf16[27,12,384]{2,1,0:T(8,128)(2,1)S(1)} collective-permute-done((bf16[27,12,384]{2,1,0:T(8,128)(2,1)S(1)}, bf16[27,12,384]{2,1,0:T(8,128)(2,1)S(1)}, u32[]{:S(2)}, u32[]{:S(2)}) %collective-permute-start.14) | collective-permute-done | bytes 248864 | tf_op jit(solution)/shard_map/ppermute | solution.py:60
  109.2 1.8 collective-permute-start.15
  111.0 23.0 %collective-permute-done.15 = bf16[27,24,384]{2,1,0:T(8,128)(2,1)S(1)} collective-permute-done((bf16[27,24,384]{2,1,0:T(8,128)(2,1)S(1)}, bf16[27,24,384]{2,1,0:T(8,128)(2,1)S(1)}, u32[]{:S(2)}, u32[]{:S(2)}) %collective-permute-start.15) | collective-permute-done | bytes 497696 | tf_op jit(solution)/shard_map/ppermute | solution.py:60
  134.3 2.5 collective-permute-start.16
  136.8 46.0 %collective-permute-done.16 = bf16[27,48,384]{2,1,0:T(8,128)(2,1)S(1)} collective-permute-done((bf16[27,48,384]{2,1,0:T(8,128)(2,1)S(1)}, bf16[27,48,384]{2,1,0:T(8,128)(2,1)S(1)}, u32[]{:S(2)}, u32[]{:S(2)}) %collective-permute-start.16) | collective-permute-done | bytes 995360 | tf_op jit(solution)/shard_map/ppermute | solution.py:60
  182.8 1.9 maximum_select_fusion.1
  185.3 3.2 collective-permute-start
  189.3 2.9 collective-permute-done
  192.2 3.1 collective-permute-start.1
  198.4 2.1 collective-permute-done.2
  201.3 1.9 collective-permute-start.3
  203.2 5.5 %collective-permute-start.8 = (bf16[6,10,1,384]{3,2,1,0:T(2,128)(2,1)}, bf16[6,10,1,384]{3,2,1,0:T(2,128)(2,1)S(1)}, u32[]{:S(2)}, u32[]{:S(2)}) collective-permute-start(bf16[6,10,1,384]{3,2,1,0:T(2,128)(2,1)} %get-tuple-element.48), channel_id=1, source_target_pairs={{1,0},{2,1},{3,2},{4,3},{5,4},{6,5},{7,6},{8,7},{9,8},{10,9},{11,1... | collective-permute-start | bytes 138248 | tf_op jit(solution)/shard_map/ppermute | solution.py:21
  214.7 2.2 fusion.32
  216.9 1.8 reshape.197
  229.5 1.8 reshape.208
  238.6 2.1 fusion.23
  257.4 4.3 %collective-permute-start.9 = (bf16[2,8,10,384]{3,2,1,0:T(8,128)(2,1)S(1)}, bf16[2,8,10,384]{3,2,1,0:T(8,128)(2,1)S(1)}, u32[]{:S(2)}, u32[]{:S(2)}) collective-permute-start(bf16[2,8,10,384]{3,2,1,0:T(8,128)(2,1)S(1)} %slice.566), channel_id=1, source_target_pairs={{0,64},{64,128},{128,192},{1,65},{65,129},{129,193},{2,66},{66,130... | collective-permute-start | bytes 368648 | tf_op jit(solution)/shard_map/ppermute | solution.py:10
  261.7 4.5 %collective-permute-done.9 = bf16[2,8,10,384]{3,2,1,0:T(8,128)(2,1)S(1)} collective-permute-done((bf16[2,8,10,384]{3,2,1,0:T(8,128)(2,1)S(1)}, bf16[2,8,10,384]{3,2,1,0:T(8,128)(2,1)S(1)}, u32[]{:S(2)}, u32[]{:S(2)}) %collective-permute-start.9) | collective-permute-done | bytes 122912 | tf_op jit(solution)/shard_map/ppermute | solution.py:10
  266.3 3.3 collective-permute-start.10
  272.8 1.8 collective-permute-done.11
  277.1 1.9 collective-permute-start.12
  279.0 3.5 %collective-permute-start.17 = (bf16[6,10,1,384]{3,2,1,0:T(2,128)(2,1)}, bf16[6,10,1,384]{3,2,1,0:T(2,128)(2,1)}, u32[]{:S(2)}, u32[]{:S(2)}) collective-permute-start(bf16[6,10,1,384]{3,2,1,0:T(2,128)(2,1)} %get-tuple-element.26), channel_id=1, source_target_pairs={{1,0},{2,1},{3,2},{4,3},{5,4},{6,5},{7,6},{8,7},{9,8},{10,9},{11,1... | collective-permute-start | bytes 138248 | tf_op jit(solution)/shard_map/ppermute | solution.py:21
  296.8 2.0 fusion.30
  298.9 1.9 reshape.227
  316.7 1.8 reshape.242
  (228 shorter events, 112.6 us)
Async XLA Ops:
  6.5 90.1 %copy-start.29 = (bf16[27,6,384]{2,0,1:T(8,128)(2,1)S(1)}, bf16[27,6,384]{2,0,1:T(8,128)(2,1)}, u32[]{:S(2)}) copy-start(bf16[27,6,384]{2,0,1:T(8,128)(2,1)} %param.12) | copy-start | bytes 373252
  6.5 230.5 %all-gather.3.cloned.1.call-start = ((), (), s32[]{:S(2)}) async-start(), calls=%async_computation | async-start | bytes 9953280 | tf_op jit(solution)/shard_map/all_gather | solution.py:67
  7.5 4.4 %collective-permute-start.4 = (bf16[27,6,384]{2,1,0:T(8,128)(2,1)S(1)}, bf16[27,6,384]{2,1,0:T(8,128)(2,1)S(1)}, u32[]{:S(2)}, u32[]{:S(2)}) collective-permute-start(bf16[27,6,384]{2,1,0:T(8,128)(2,1)S(1)} %copy.12), channel_id=1, source_target_pairs={{0,1},{1,0},{2,3},{3,2},{4,5},{5,4},{6,7},{7,6},{8,9},{9,8},{10,11... | collective-permute-start | bytes 373256 | tf_op jit(solution)/shard_map/ppermute | solution.py:60
  12.1 9.1 %collective-permute-start.5 = (bf16[27,12,384]{2,1,0:T(8,128)(2,1)S(1)}, bf16[27,12,384]{2,1,0:T(8,128)(2,1)S(1)}, u32[]{:S(2)}, u32[]{:S(2)}) collective-permute-start(bf16[27,12,384]{2,1,0:T(8,128)(2,1)S(1)} %maximum_select_fusion.6), channel_id=1, source_target_pairs={{0,2},{1,3},{2,0},{3,1},{4,6},{5,7},{6,4},{7,5},{8,10},{9,11},{10,... | collective-permute-start | bytes 746504 | tf_op jit(solution)/shard_map/ppermute | solution.py:60
  21.5 24.6 %collective-permute-start.6 = (bf16[27,24,384]{2,1,0:T(8,128)(2,1)S(1)}, bf16[27,24,384]{2,1,0:T(8,128)(2,1)S(1)}, u32[]{:S(2)}, u32[]{:S(2)}) collective-permute-start(bf16[27,24,384]{2,1,0:T(8,128)(2,1)S(1)} %maximum_select_fusion.4), channel_id=1, source_target_pairs={{0,4},{1,5},{2,6},{3,7},{4,0},{5,1},{6,2},{7,3},{8,12},{9,13},{10,... | collective-permute-start | bytes 1493000 | tf_op jit(solution)/shard_map/ppermute | solution.py:60
  46.5 48.2 %collective-permute-start.7 = (bf16[27,48,384]{2,1,0:T(8,128)(2,1)S(1)}, bf16[27,48,384]{2,1,0:T(8,128)(2,1)S(1)}, u32[]{:S(2)}, u32[]{:S(2)}) collective-permute-start(bf16[27,48,384]{2,1,0:T(8,128)(2,1)S(1)} %maximum_select_fusion.2), channel_id=1, source_target_pairs={{0,8},{1,9},{2,10},{3,11},{4,12},{5,13},{6,14},{7,15},{8,0},{9,1},... | collective-permute-start | bytes 2985992 | tf_op jit(solution)/shard_map/ppermute | solution.py:60
  51.6 133.2 %copy-start.1 = (bf16[4,8,10,384]{3,1,2,0:T(8,128)(2,1)S(1)}, bf16[4,8,10,384]{3,1,2,0:T(8,128)(2,1)}, u32[]{:S(2)}) copy-start(bf16[4,8,10,384]{3,1,2,0:T(8,128)(2,1)} %param.7) | copy-start | bytes 737284
  51.6 133.3 %copy-start.31 = (f32[384]{0:T(512)S(1)}, f32[384]{0:T(512)}, u32[]{:S(2)}) copy-start(f32[384]{0:T(512)} %param.8) | copy-start | bytes 4612
  96.6 187.1 %all-gather.5.cloned.1.call-start = ((), (), s32[]{:S(2)}) async-start(), calls=%async_computation.1 | async-start | bytes 9953280 | tf_op jit(solution)/shard_map/all_gather | solution.py:67
  96.7 2.9 collective-permute-start.13
  99.8 9.1 %collective-permute-start.14 = (bf16[27,12,384]{2,1,0:T(8,128)(2,1)S(1)}, bf16[27,12,384]{2,1,0:T(8,128)(2,1)S(1)}, u32[]{:S(2)}, u32[]{:S(2)}) collective-permute-start(bf16[27,12,384]{2,1,0:T(8,128)(2,1)S(1)} %maximum_select_fusion.7), channel_id=1, source_target_pairs={{0,2},{1,3},{2,0},{3,1},{4,6},{5,7},{6,4},{7,5},{8,10},{9,11},{10,... | collective-permute-start | bytes 746504 | tf_op jit(solution)/shard_map/ppermute | solution.py:60
  109.2 24.8 %collective-permute-start.15 = (bf16[27,24,384]{2,1,0:T(8,128)(2,1)S(1)}, bf16[27,24,384]{2,1,0:T(8,128)(2,1)S(1)}, u32[]{:S(2)}, u32[]{:S(2)}) collective-permute-start(bf16[27,24,384]{2,1,0:T(8,128)(2,1)S(1)} %maximum_select_fusion.5), channel_id=1, source_target_pairs={{0,4},{1,5},{2,6},{3,7},{4,0},{5,1},{6,2},{7,3},{8,12},{9,13},{10,... | collective-permute-start | bytes 1493000 | tf_op jit(solution)/shard_map/ppermute | solution.py:60
  134.3 48.5 %collective-permute-start.16 = (bf16[27,48,384]{2,1,0:T(8,128)(2,1)S(1)}, bf16[27,48,384]{2,1,0:T(8,128)(2,1)S(1)}, u32[]{:S(2)}, u32[]{:S(2)}) collective-permute-start(bf16[27,48,384]{2,1,0:T(8,128)(2,1)S(1)} %maximum_select_fusion.3), channel_id=1, source_target_pairs={{0,8},{1,9},{2,10},{3,11},{4,12},{5,13},{6,14},{7,15},{8,0},{9,1},... | collective-permute-start | bytes 2985992 | tf_op jit(solution)/shard_map/ppermute | solution.py:60
  185.3 6.9 %collective-permute-start = (bf16[2,8,10,384]{3,2,1,0:T(8,128)(2,1)S(1)}, bf16[2,8,10,384]{3,2,1,0:T(8,128)(2,1)S(1)}, u32[]{:S(2)}, u32[]{:S(2)}) collective-permute-start(bf16[2,8,10,384]{3,2,1,0:T(8,128)(2,1)S(1)} %slice.512), channel_id=1, source_target_pairs={{0,64},{64,128},{128,192},{1,65},{65,129},{129,193},{2,66},{66,130... | collective-permute-start | bytes 368648 | tf_op jit(solution)/shard_map/ppermute | solution.py:10
  192.2 6.2 %collective-permute-start.1 = (bf16[6,1,10,384]{3,2,1,0:T(8,128)(2,1)S(1)}, bf16[6,1,10,384]{3,2,1,0:T(8,128)(2,1)S(1)}, u32[]{:S(2)}, u32[]{:S(2)}) collective-permute-start(bf16[6,1,10,384]{3,2,1,0:T(8,128)(2,1)S(1)} %get-tuple-element.71), channel_id=1, source_target_pairs={{0,16},{16,32},{32,48},{1,17},{17,33},{33,49},{2,18},{18,34},{34,5... | collective-permute-start | bytes 138248 | tf_op jit(solution)/shard_map/ppermute | solution.py:20
  195.4 5.1 %collective-permute-start.2 = (bf16[6,1,10,384]{3,2,1,0:T(8,128)(2,1)S(1)}, bf16[6,1,10,384]{3,2,1,0:T(8,128)(2,1)S(1)}, u32[]{:S(2)}, u32[]{:S(2)}) collective-permute-start(bf16[6,1,10,384]{3,2,1,0:T(8,128)(2,1)S(1)} %get-tuple-element.72), channel_id=1, source_target_pairs={{16,0},{32,16},{48,32},{17,1},{33,17},{49,33},{18,2},{34,18},{50,3... | collective-permute-start | bytes 138248 | tf_op jit(solution)/shard_map/ppermute | solution.py:21
  201.3 12.8 %collective-permute-start.3 = (bf16[6,10,1,384]{3,2,1,0:T(2,128)(2,1)}, bf16[6,10,1,384]{3,2,1,0:T(2,128)(2,1)S(1)}, u32[]{:S(2)}, u32[]{:S(2)}) collective-permute-start(bf16[6,10,1,384]{3,2,1,0:T(2,128)(2,1)} %get-tuple-element.47), channel_id=1, source_target_pairs={{0,1},{1,2},{2,3},{3,4},{4,5},{5,6},{6,7},{7,8},{8,9},{9,10},{10,1... | collective-permute-start | bytes 138248 | tf_op jit(solution)/shard_map/ppermute | solution.py:20
  203.2 10.8 %collective-permute-start.8 = (bf16[6,10,1,384]{3,2,1,0:T(2,128)(2,1)}, bf16[6,10,1,384]{3,2,1,0:T(2,128)(2,1)S(1)}, u32[]{:S(2)}, u32[]{:S(2)}) collective-permute-start(bf16[6,10,1,384]{3,2,1,0:T(2,128)(2,1)} %get-tuple-element.48), channel_id=1, source_target_pairs={{1,0},{2,1},{3,2},{4,3},{5,4},{6,5},{7,6},{8,7},{9,8},{10,9},{11,1... | collective-permute-start | bytes 138248 | tf_op jit(solution)/shard_map/ppermute | solution.py:21
  235.6 12.6 %copy-start.14 = (bf16[320,384]{1,0:T(8,128)(2,1)S(1)}, bf16[320,384]{1,0:T(8,128)(2,1)}, u32[]{:S(2)}) copy-start(bf16[320,384]{1,0:T(8,128)(2,1)} %reshape.204) | copy-start | bytes 737284
  237.0 14.2 %copy-start.12 = (bf16[320,384]{1,0:T(8,128)(2,1)S(1)}, bf16[320,384]{1,0:T(8,128)(2,1)}, u32[]{:S(2)}) copy-start(bf16[320,384]{1,0:T(8,128)(2,1)} %reshape.207) | copy-start | bytes 737284
  238.6 12.9 %copy-start.20 = (bf16[320,384]{1,0:T(8,128)(2,1)S(1)}, bf16[320,384]{1,0:T(8,128)(2,1)}, u32[]{:S(2)}) copy-start(bf16[320,384]{1,0:T(8,128)(2,1)} %reshape.208) | copy-start | bytes 737284
  257.4 8.8 %collective-permute-start.9 = (bf16[2,8,10,384]{3,2,1,0:T(8,128)(2,1)S(1)}, bf16[2,8,10,384]{3,2,1,0:T(8,128)(2,1)S(1)}, u32[]{:S(2)}, u32[]{:S(2)}) collective-permute-start(bf16[2,8,10,384]{3,2,1,0:T(8,128)(2,1)S(1)} %slice.566), channel_id=1, source_target_pairs={{0,64},{64,128},{128,192},{1,65},{65,129},{129,193},{2,66},{66,130... | collective-permute-start | bytes 368648 | tf_op jit(solution)/shard_map/ppermute | solution.py:10
  266.3 6.5 %collective-permute-start.10 = (bf16[6,1,10,384]{3,2,1,0:T(8,128)(2,1)S(1)}, bf16[6,1,10,384]{3,2,1,0:T(8,128)(2,1)S(1)}, u32[]{:S(2)}, u32[]{:S(2)}) collective-permute-start(bf16[6,1,10,384]{3,2,1,0:T(8,128)(2,1)S(1)} %get-tuple-element.65), channel_id=1, source_target_pairs={{0,16},{16,32},{32,48},{1,17},{17,33},{33,49},{2,18},{18,34},{34,5... | collective-permute-start | bytes 138248 | tf_op jit(solution)/shard_map/ppermute | solution.py:20
  269.5 5.1 %collective-permute-start.11 = (bf16[6,1,10,384]{3,2,1,0:T(8,128)(2,1)S(1)}, bf16[6,1,10,384]{3,2,1,0:T(8,128)(2,1)S(1)}, u32[]{:S(2)}, u32[]{:S(2)}) collective-permute-start(bf16[6,1,10,384]{3,2,1,0:T(8,128)(2,1)S(1)} %get-tuple-element.66), channel_id=1, source_target_pairs={{16,0},{32,16},{48,32},{17,1},{33,17},{49,33},{18,2},{34,18},{50,3... | collective-permute-start | bytes 138248 | tf_op jit(solution)/shard_map/ppermute | solution.py:21
  277.1 14.7 %collective-permute-start.12 = (bf16[6,10,1,384]{3,2,1,0:T(2,128)(2,1)}, bf16[6,10,1,384]{3,2,1,0:T(2,128)(2,1)}, u32[]{:S(2)}, u32[]{:S(2)}) collective-permute-start(bf16[6,10,1,384]{3,2,1,0:T(2,128)(2,1)} %get-tuple-element.25), channel_id=1, source_target_pairs={{0,1},{1,2},{2,3},{3,4},{4,5},{5,6},{6,7},{7,8},{8,9},{9,10},{10,1... | collective-permute-start | bytes 138248 | tf_op jit(solution)/shard_map/ppermute | solution.py:20
  279.0 12.8 %collective-permute-start.17 = (bf16[6,10,1,384]{3,2,1,0:T(2,128)(2,1)}, bf16[6,10,1,384]{3,2,1,0:T(2,128)(2,1)}, u32[]{:S(2)}, u32[]{:S(2)}) collective-permute-start(bf16[6,10,1,384]{3,2,1,0:T(2,128)(2,1)} %get-tuple-element.26), channel_id=1, source_target_pairs={{1,0},{2,1},{3,2},{4,3},{5,4},{6,5},{7,6},{8,7},{9,8},{10,9},{11,1... | collective-permute-start | bytes 138248 | tf_op jit(solution)/shard_map/ppermute | solution.py:21
  298.9 21.7 %copy-start.3 = (bf16[4,8,10,384]{3,2,1,0:T(8,128)(2,1)S(1)}, bf16[4,8,10,384]{3,2,1,0:T(8,128)(2,1)}, u32[]{:S(2)}) copy-start(bf16[4,8,10,384]{3,2,1,0:T(8,128)(2,1)} %get-tuple-element.6) | copy-start | bytes 737284
  298.9 21.9 %copy-start.2 = (bf16[4,8,10,384]{3,2,1,0:T(8,128)(2,1)S(1)}, bf16[4,8,10,384]{3,2,1,0:T(8,128)(2,1)}, u32[]{:S(2)}) copy-start(bf16[4,8,10,384]{3,2,1,0:T(8,128)(2,1)} %get-tuple-element.5) | copy-start | bytes 737284
  320.6 15.1 %copy-start.13 = (bf16[320,384]{1,0:T(8,128)(2,1)S(1)}, bf16[320,384]{1,0:T(8,128)(2,1)}, u32[]{:S(2)}) copy-start(bf16[320,384]{1,0:T(8,128)(2,1)} %reshape.235) | copy-start | bytes 737284
  320.9 16.1 %slice-start = ((s8[7962624]{0:T(1024)(128)(4,1)}), s8[4194304]{0:T(1024)(128)(4,1)S(1)}, s32[]{:S(2)}) async-start(s8[7962624]{0:T(1024)(128)(4,1)} %bitcast.217), calls=%async_computation.2 | async-start | bytes 8388608
  320.9 16.1 %copy-start.23 = (bf16[320,384]{1,0:T(8,128)(2,1)S(1)}, bf16[320,384]{1,0:T(8,128)(2,1)}, u32[]{:S(2)}) copy-start(bf16[320,384]{1,0:T(8,128)(2,1)} %reshape.236) | copy-start | bytes 737284
  323.9 13.5 %copy-start.22 = (bf16[320,384]{1,0:T(8,128)(2,1)S(1)}, bf16[320,384]{1,0:T(8,128)(2,1)}, u32[]{:S(2)}) copy-start(bf16[320,384]{1,0:T(8,128)(2,1)} %reshape.237) | copy-start | bytes 737284
  (24 other events, 171.3 us)
Sparse Core Ops, SparseCore 0:
  96.7 81.8 all-gather.2
  184.8 81.4 all-gather.4
